TPU v7x, 32 devices: a whole 2x2x4 slice. The times are simulated.
32 devices in a mesh: pipe: 8 (over z, x), tensor: 4 (over y, core).
Axes of the slice: x: 2, y: 2, z: 4, core: 2. Of those that a mesh axis runs over, the one named last changes fastest.
Arguments:
- x_saved: bfloat16 [8, 2, 4096, 128], P('pipe', None, 'tensor'), may hold values from -6 to 6
- seed_grad: bfloat16 [8, 2, 4096, 128], P('pipe', None, 'tensor'), may hold values from -6 to 6
- gate_blocks: bfloat16 [8, 4, 7, 20, 4096], P('pipe', 'tensor'), may hold values from -0.1875 to 0.1875
- up_blocks: bfloat16 [8, 4, 7, 20, 4096], P('pipe', 'tensor'), may hold values from -0.1875 to 0.1875
- down_blocks: bfloat16 [8, 4, 7, 20, 4096], P('pipe', 'tensor'), may hold values from -0.1875 to 0.1875
- gate_rows: int32 [8, 4, 7, 20], P('pipe', 'tensor'), may hold values from -1 to 63, as said below
- down_rows: int32 [8, 4, 7, 20], P('pipe', 'tensor'), may hold values from -1 to 63, as said below
Outputs:
- grad_input: bfloat16 [8, 2, 4096, 128], P('pipe', None, 'tensor')
Inputs may be any that keep to these rules, and one draw needn't show every extreme that they name: `gate_rows`: in one column of tiles the non-negative entries are distinct and come before the -1 entries. All columns of one tensor shard of one section hold the same number of kept tiles, from 12 to 20, and in every section one shard holds 20 in every column. `down_rows`: as for gate_rows, drawn independently.
All inputs are finite; a program needn't handle non-finite values.
Results may differ from a plain program's by a relative error of at most 0.007.
Values may be sent and summed in bfloat16 or wider, within the bound.
A program may use at most 128 MiB of HBM per device.

v0:
```python
import jax
import jax.numpy as jnp
from jax import lax
from jax.sharding import PartitionSpec as P

BLK = 64


def partner_2(x, axis, distance):
    return lax.ppermute(x, axis, [(i, i ^ 1 << distance) for i in range(lax.axis_size(axis))])


def from_behind(block, axis, distance):
    devices = range(lax.axis_size(axis))
    route = [(i - distance, i) for i in devices if i - distance in devices]
    return lax.ppermute(block, axis, route)


def gather_tiles(source, row_ids):
    columns, slot_depth = row_ids.shape
    filled = (row_ids >= 0).reshape(-1)
    picked = jnp.take(source, jnp.maximum(row_ids, 0).reshape(-1), axis=0)
    picked = jnp.where(filled[:, None, None], picked, jnp.zeros_like(picked))
    return picked.reshape(columns, slot_depth, source.shape[1], source.shape[2])


def layer_branch(x_full, cot_full, paired_grid, down_grid, gate_ids, down_ids):
    row_blocks = x_full.shape[0] // BLK
    tokens_now = x_full.shape[1]
    columns, slot_depth = gate_ids.shape
    x_picked = gather_tiles(x_full.reshape(row_blocks, BLK, tokens_now), gate_ids)
    both_values = jnp.einsum(
        "crkj,crkt->cjt", paired_grid, x_picked, preferred_element_type=jnp.float32
    )
    gate_value = both_values[:, :BLK]
    up_value = both_values[:, BLK:]
    cot_picked = gather_tiles(cot_full.reshape(row_blocks, BLK, tokens_now), down_ids)
    d_hidden = jnp.einsum(
        "crjk,crkt->cjt", down_grid, cot_picked, preferred_element_type=jnp.float32
    )
    sigmoid_gate = jax.nn.sigmoid(gate_value)
    d_gate = (
        d_hidden * up_value * sigmoid_gate * (1.0 + gate_value * (1.0 - sigmoid_gate))
    ).astype(jnp.bfloat16)
    d_up = (d_hidden * gate_value * sigmoid_gate).astype(jnp.bfloat16)
    d_both = jnp.concatenate([d_gate, d_up], axis=1)
    per_slot = jnp.einsum("crkj,cjt->crkt", paired_grid, d_both, preferred_element_type=jnp.float32)
    segment_ids = jnp.where(gate_ids >= 0, gate_ids, row_blocks).reshape(-1)
    summed = jax.ops.segment_sum(
        per_slot.reshape(columns * slot_depth, BLK, tokens_now),
        segment_ids,
        num_segments=row_blocks + 1,
    )
    return summed[:row_blocks].reshape(row_blocks * BLK, tokens_now)


def per_device(x_saved, seed_grad, gate_blocks, up_blocks, down_blocks, gate_rows, down_rows):
    pipe_index = lax.axis_index("pipe")
    pair_half = pipe_index % 2
    last_section = pipe_index // 2 == lax.axis_size("pipe") // 2 - 1
    own_parts = (gate_blocks, up_blocks, down_blocks, gate_rows, down_rows)
    partner = partner_2((gate_blocks, up_blocks, down_blocks, gate_rows, down_rows), "pipe", 0)
    joined = []
    for own_part, theirs in zip(own_parts, partner):
        first_half = jnp.where(pair_half == 0, own_part, theirs)
        second_half = jnp.where(pair_half == 0, theirs, own_part)
        joined.append(jnp.concatenate([first_half[0, 0], second_half[0, 0]], axis=0))
    gate_set, up_set, down_set, gate_ids, down_ids = joined
    columns, slot_depth = gate_ids.shape
    tile_shape = (columns, slot_depth, BLK, BLK)
    paired_grid = jnp.concatenate(
        [gate_set.reshape(tile_shape), up_set.reshape(tile_shape)], axis=3
    )
    down_grid = down_set.reshape(tile_shape)
    panel_rows = x_saved.shape[2]
    micro_total = x_saved.shape[1]
    arrived = None
    grads = []
    for micro_step in range(micro_total):
        x_panel = x_saved[0, micro_step]
        seed_panel = seed_grad[0, micro_step]
        x_full, cot_full = (
            lax.all_gather(x_panel, "tensor", axis=0, tiled=True),
            lax.all_gather(seed_panel, "tensor", axis=0, tiled=True),
        )
        if micro_step > 0:
            cot_full = jnp.where(last_section, cot_full, arrived)
        branch = layer_branch(x_full, cot_full, paired_grid, down_grid, gate_ids, down_ids)
        summed = lax.psum(branch, "tensor")
        grad_full = (cot_full.astype(jnp.float32) + summed).astype(jnp.bfloat16)
        grad_panel = lax.dynamic_slice_in_dim(
            grad_full, lax.axis_index("tensor") * panel_rows, panel_rows, 0
        )
        if micro_step + 1 < micro_total:
            arrived = from_behind(grad_full, "pipe", -2)
        grads.append(grad_panel)
    return jnp.stack(grads)[None]


def solution(mesh):
    return jax.shard_map(
        per_device,
        mesh=mesh,
        in_specs=(
            P("pipe", None, "tensor", None),
            P("pipe", None, "tensor", None),
            P("pipe", "tensor", None, None, None),
            P("pipe", "tensor", None, None, None),
            P("pipe", "tensor", None, None, None),
            P("pipe", "tensor", None, None),
            P("pipe", "tensor", None, None),
        ),
        out_specs=P("pipe", None, "tensor", None),
        check_vma=False,
    )
```

profile of v0, /device:TPU:0, one launch (start us, length us, event | category | flops | bytes accessed | tf_op | source)
XLA Modules:
  0.0 393.3 jit_solution(10879829134732168787)
XLA Ops:
  6.5 1.9 fusion.43
  8.5 0.7 all-gather.11.cloned.1.call-update
  9.2 0.7 copy.21
  9.9 2.9 collective-permute-start
  12.9 2.0 collective-permute-start.3
  14.9 2.0 collective-permute-start.1
  16.9 1.9 fusion.44
  18.9 0.7 select_bitcast_fusion.1
  20.3 24.5 %collective-permute-done.3 = bf16[1,1,7,20,4096]{4,2,3,1,0:T(8,128)(2,1)S(1)} collective-permute-done((bf16[1,1,7,20,4096]{4,2,3,1,0:T(8,128)(2,1)}, bf16[1,1,7,20,4096]{4,2,3,1,0:T(8,128)(2,1)S(1)}, u32[]{:S(2)}, u32[]{:S(2)}) %collective-permute-start.3) | collective-permute-done | bytes 1146912 | tf_op jit(solution)/shard_map/ppermute | solution.py:10
  44.8 28.1 %collective-permute-done.2 = bf16[1,1,7,20,4096]{4,2,3,1,0:T(8,128)(2,1)S(1)} collective-permute-done((bf16[1,1,7,20,4096]{4,2,3,1,0:T(8,128)(2,1)}, bf16[1,1,7,20,4096]{4,2,3,1,0:T(8,128)(2,1)S(1)}, u32[]{:S(2)}, u32[]{:S(2)}) %collective-permute-start.2) | collective-permute-done | bytes 1146912 | tf_op jit(solution)/shard_map/ppermute | solution.py:10
  72.9 4.2 %broadcast_select_fusion.1 = (bf16[1,1,7,20,4096]{4,2,3,1,0:T(8,128)(2,1)}, bf16[1,1,7,20,4096]{4,2,3,1,0:T(8,128)(2,1)}, bf16[1,1,7,20,4096]{4,2,3,1,0:T(8,128)(2,1)}, bf16[1,1,7,20,4096]{4,2,3,1,0:T(8,128)(2,1)}) fusion(bf16[1,1,7,20,4096]{4,2,3,1,0:T(8,128)(2,1)} %param.13, bf16[1,1,7,20,4096]{4,2,3,1,0:T(8,128)(2,1)S(1)} %collective-permute-done.3, ...), kind=kLoop, calls=%fused_computation.29 | loop fusion | flops 2293760 | bytes 9175041 | tf_op jit(solution)/shard_map/jit(_where)/select_n | solution.py:65
  77.1 3.6 concatenate.47
  80.7 4.5 %concatenate.46 = bf16[7,20,64,64]{3,2,0,1:T(8,128)(2,1)} reshape(bf16[1,1,7,20,4096]{4,2,3,1,0:T(8,128)(2,1)} %get-tuple-element.27) | data formatting | bytes 2293760 | tf_op jit(solution)/shard_map/concatenate | solution.py:67
  85.2 14.4 %collective-permute-done.1 = bf16[1,1,7,20,4096]{4,2,3,1,0:T(8,128)(2,1)} collective-permute-done((bf16[1,1,7,20,4096]{4,2,3,1,0:T(8,128)(2,1)}, bf16[1,1,7,20,4096]{4,2,3,1,0:T(8,128)(2,1)}, u32[]{:S(2)}, u32[]{:S(2)}) %collective-permute-start.1) | collective-permute-done | bytes 1146912 | tf_op jit(solution)/shard_map/ppermute | solution.py:10
  99.7 3.3 broadcast_select_fusion.5
  103.0 4.5 %concatenate.44 = bf16[7,20,64,64]{3,2,0,1:T(8,128)(2,1)} reshape(bf16[1,1,7,20,4096]{4,2,3,1,0:T(8,128)(2,1)} %get-tuple-element.9) | data formatting | bytes 2293760 | tf_op jit(solution)/shard_map/concatenate | solution.py:67
  107.6 4.5 %concatenate.43 = bf16[7,20,64,64]{3,2,0,1:T(8,128)(2,1)} reshape(bf16[1,1,7,20,4096]{4,2,3,1,0:T(8,128)(2,1)} %get-tuple-element.8) | data formatting | bytes 2293760 | tf_op jit(solution)/shard_map/concatenate | solution.py:67
  112.1 4.5 %concatenate.51 = bf16[7,20,64,64]{3,2,0,1:T(8,128)(2,1)} reshape(bf16[1,1,7,20,4096]{4,2,3,1,0:T(8,128)(2,1)} %get-tuple-element.7) | data formatting | bytes 2293760 | tf_op jit(solution)/shard_map/concatenate | solution.py:67
  116.6 4.5 %concatenate.50 = bf16[7,20,64,64]{3,2,0,1:T(8,128)(2,1)} reshape(bf16[1,1,7,20,4096]{4,2,3,1,0:T(8,128)(2,1)} %get-tuple-element.6) | data formatting | bytes 2293760 | tf_op jit(solution)/shard_map/concatenate | solution.py:67
  121.1 6.3 %maximum_maximum_fusion = bf16[14,20,64,128]{3,2,0,1:T(8,128)(2,1)} fusion(bf16[7,20,64,64]{3,2,0,1:T(8,128)(2,1)S(1)} %concatenate.47, bf16[7,20,64,64]{3,2,0,1:T(8,128)(2,1)} %concatenate.46, bf16[7,20,64,64]{3,2,0,1:T(8,128)(2,1)} %concatenate.44, bf16[7,20,64,64]{3,2,0,1:T(8,128)(2,1)} %concatenate.43), kind=kLoop, calls=%fused_computation.6 | loop fusion | flops 18350080 | bytes 9175040 | tf_op jit(solution)/shard_map/concatenate | solution.py:71
  127.5 4.6 %gather_fusion.3 = bf16[280,64,128]{2,1,0:T(8,128)(2,1)} fusion(bf16[64,64,128]{2,1,0:T(8,128)(2,1)} %bitcast.80, s32[1024]{0:T(1024)S(1)} %pad_clamp_fusion), kind=kCustom, calls=%fused_computation.3.clone | custom fusion | bytes 9176160 | tf_op jit(solution)/shard_map/jit(_take)/gather | solution.py:22
  132.1 4.7 %gather_fusion.1 = bf16[280,64,128]{2,1,0:T(8,128)(2,1)} fusion(bf16[64,64,128]{2,1,0:T(8,128)(2,1)} %bitcast.81, s32[1024]{0:T(1024)S(1)} %pad_clamp_fusion), kind=kCustom, calls=%fused_computation.1.clone | custom fusion | bytes 9176160 | tf_op jit(solution)/shard_map/jit(_take)/gather | solution.py:22
  136.8 7.8 %select_select_fusion = (bf16[280,64,128]{2,1,0:T(8,128)(2,1)}, bf16[280,64,128]{2,1,0:T(8,128)(2,1)S(1)}) fusion(bf16[280,64,128]{2,1,0:T(8,128)(2,1)} %gather_fusion.3, pred[280]{0:T(512)(128)(4,1)S(1)} %compare_and_fusion, pred[280]{0:T(512)(128)(4,1)S(1)} %ge.42, bf16[280,64,128]{2,1,0:T(8,128)(2,1)} %gather_fusion.1), kind=kLoop, calls=%fused_computation.8 | loop fusion | flops 9175040 | bytes 18350640 | tf_op jit(solution)/shard_map/jit(_where)/select_n | solution.py:23
  144.6 1.5 fusion.13
  146.2 4.7 %gather_fusion = bf16[280,64,128]{2,1,0:T(8,128)(2,1)} fusion(bf16[64,64,128]{2,1,0:T(8,128)(2,1)} %bitcast.79, s32[1024]{0:T(1024)S(1)} %pad_clamp_fusion.1), kind=kCustom, calls=%fused_computation.clone | custom fusion | bytes 9176160 | tf_op jit(solution)/shard_map/jit(_take)/gather | solution.py:22
  150.8 4.7 %select_select_fusion.3 = bf16[280,64,128]{2,1,0:T(8,128)(2,1)S(1)} fusion(bf16[280,64,128]{2,1,0:T(8,128)(2,1)} %gather_fusion, pred[280]{0:T(512)(128)(4,1)S(1)} %compare_and_fusion.1, pred[280]{0:T(512)(128)(4,1)S(1)} %ge.40), kind=kLoop, calls=%fused_computation.11 | loop fusion | flops 4587520 | bytes 9175600 | tf_op jit(solution)/shard_map/jit(_where)/select_n | solution.py:23
  155.6 2.0 fusion.31
  157.6 4.9 %fusion.8 = f32[14,20,64,128]{3,2,1,0:T(8,128)} fusion(bf16[14,20,64,128]{3,2,0,1:T(8,128)(2,1)S(1)} %bitcast.73, bf16[14,64,128]{2,1,0:T(8,128)(2,1)S(1)} %get-tuple-element.15, bf16[14,64,128]{2,1,0:T(8,128)(2,1)S(1)} %get-tuple-element.14), kind=kOutput, calls=%fused_computation.20 | convolution fusion | flops 588120064 | bytes 14221312 | tf_op jit(solution)/shard_map/crkj,cjt->crkt/dot_general | solution.py:47
  162.8 29.7 %scatter_fusion = f32[65,64,128]{2,1,0:T(8,128)S(1)} fusion(f32[65,64,128]{2,1,0:T(8,128)S(1)} %broadcast.48.clone, s32[280]{0:T(512)S(1)} %fusion.40, f32[280,64,128]{2,1,0:T(8,128)} %bitcast.77), kind=kCustom, calls=%fused_computation.4 | custom fusion | flops 2293760 | bytes 27526240 | tf_op jit(solution)/shard_map/scatter-add | solution.py:49
  192.6 1.5 slice.50
  194.1 0.5 all-gather.13.cloned.1.call-update
  194.7 52.4 %all-reduce.3.cloned.1.call-done = f32[4096,128]{1,0:T(8,128)} async-done(((f32[4096,128]{1,0:T(8,128)}), f32[4096,128]{1,0:T(8,128)}) %all-reduce.3.cloned.1.call-update) | async-done | bytes 2097168 | tf_op jit(solution)/shard_map/psum | solution.py:89
  247.1 1.8 fusion.12
  248.9 1.3 collective-permute-start.5
  250.2 6.1 %fusion.16 = f32[14,128,128]{2,1,0:T(8,128)} fusion(bf16[14,20,64,128]{3,2,1,0:T(8,128)(2,1)} %bitcast.84, bf16[14,20,64,128]{3,2,0,1:T(8,128)(2,1)} %maximum_maximum_fusion), kind=kOutput, calls=%fused_computation.27 | convolution fusion | flops 587202560 | bytes 10092544 | tf_op jit(solution)/shard_map/crkj,crkt->cjt/dot_general | solution.py:32
  256.3 9.1 %all-gather.13.cloned.1.call-done = bf16[1,1,4096,128]{3,2,1,0:T(8,128)(2,1)} async-done(((bf16[1,1,1024,128]{3,2,1,0:T(8,128)(2,1)}), bf16[1,1,4096,128]{3,2,1,0:T(8,128)(2,1)}) %all-gather.13.cloned.1.call-update) | async-done | bytes 1048592 | tf_op jit(solution)/shard_map/all_gather | solution.py:84
  265.4 10.2 %collective-permute-done.5 = bf16[4096,128]{1,0:T(8,128)(2,1)S(1)} collective-permute-done((bf16[4096,128]{1,0:T(8,128)(2,1)S(1)}, bf16[4096,128]{1,0:T(8,128)(2,1)S(1)}, u32[]{:S(2)}, u32[]{:S(2)}) %collective-permute-start.5) | collective-permute-done | bytes 1048608 | tf_op jit(solution)/shard_map/ppermute | solution.py:16
  275.6 1.3 bitcast_select_fusion
  277.0 13.6 %gather_fusion.2 = bf16[280,64,128]{2,1,0:T(8,128)(2,1)} fusion(bf16[64,64,128]{2,1,0:T(8,128)(2,1)S(1)} %bitcast.78, s32[1024]{0:T(1024)S(1)} %pad_clamp_fusion.1), kind=kCustom, calls=%fused_computation.2.clone | custom fusion | bytes 9176160 | tf_op jit(solution)/shard_map/jit(_take)/gather | solution.py:22
  290.6 4.7 %select_select_fusion.1 = bf16[280,64,128]{2,1,0:T(8,128)(2,1)S(1)} fusion(bf16[280,64,128]{2,1,0:T(8,128)(2,1)} %gather_fusion.2, pred[280]{0:T(512)(128)(4,1)S(1)} %compare_and_fusion.1, pred[280]{0:T(512)(128)(4,1)S(1)} %ge.40), kind=kLoop, calls=%fused_computation.9 | loop fusion | flops 4587520 | bytes 9175600 | tf_op jit(solution)/shard_map/jit(_where)/select_n | solution.py:23
  295.3 2.0 fusion.28
  297.4 4.9 %fusion.4 = f32[14,20,64,128]{3,2,1,0:T(8,128)} fusion(bf16[14,20,64,128]{3,2,0,1:T(8,128)(2,1)S(1)} %bitcast.75, bf16[14,64,128]{2,1,0:T(8,128)(2,1)S(1)} %get-tuple-element.13, bf16[14,64,128]{2,1,0:T(8,128)(2,1)S(1)} %get-tuple-element.12), kind=kOutput, calls=%fused_computation.16 | convolution fusion | flops 588120064 | bytes 14221312 | tf_op jit(solution)/shard_map/crkj,cjt->crkt/dot_general | solution.py:47
  302.6 29.7 %scatter_fusion.1 = f32[65,64,128]{2,1,0:T(8,128)S(1)} fusion(f32[65,64,128]{2,1,0:T(8,128)S(1)} %broadcast.48, s32[280]{0:T(512)S(1)} %fusion.40, f32[280,64,128]{2,1,0:T(8,128)} %bitcast.76), kind=kCustom, calls=%fused_computation.5 | custom fusion | flops 2293760 | bytes 27526240 | tf_op jit(solution)/shard_map/scatter-add | solution.py:49
  332.3 1.5 slice.53
  333.8 1.0 dynamic-slice_bitcast_fusion
  334.8 49.8 %all-reduce.5.cloned.1.call-done = f32[4096,128]{1,0:T(8,128)} async-done(((f32[4096,128]{1,0:T(8,128)}), f32[4096,128]{1,0:T(8,128)}) %all-reduce.5.cloned.1.call-update) | async-done | bytes 2097168 | tf_op jit(solution)/shard_map/psum | solution.py:89
  384.6 1.1 fusion.36
  385.7 0.8 maximum_bitcast_fusion
  (66 shorter events, 1.5 us)
Async XLA Ops:
  6.5 120.9 %all-gather.15.cloned.1.call-start = ((), (), s32[]{:S(2)}) async-start(), calls=%async_computation.5 | async-start | bytes 1310720 | tf_op jit(solution)/shard_map/all_gather | solution.py:83
  8.4 123.7 %all-gather.11.cloned.1.call-start = ((), (), s32[]{:S(2)}) async-start(), calls=%async_computation.3 | async-start | bytes 1310720 | tf_op jit(solution)/shard_map/all_gather | solution.py:83
  9.2 137.0 %all-gather.9.cloned.1.call-start = ((), (), s32[]{:S(2)}) async-start(), calls=%async_computation.2 | async-start | bytes 1310720 | tf_op jit(solution)/shard_map/all_gather | solution.py:84
  9.9 9.0 %collective-permute-start = (s32[1,1,7,20]{3,2,1,0:T(8,128)S(1)}, s32[1,1,7,20]{3,2,1,0:T(8,128)S(1)}, u32[]{:S(2)}, u32[]{:S(2)}) collective-permute-start(s32[1,1,7,20]{3,2,1,0:T(8,128)S(1)} %copy.21), channel_id=1, source_target_pairs={{0,4},{4,0},{8,12},{12,8},{16,20},{20,16},{24,28},{28,24},{1,5},{5... | collective-permute-start | bytes 1688 | tf_op jit(solution)/shard_map/ppermute | solution.py:10
  12.8 6.1 %collective-permute-start.4 = (s32[1,1,7,20]{3,1,2,0:T(1,128)}, s32[1,1,7,20]{3,1,2,0:T(1,128)S(1)}, u32[]{:S(2)}, u32[]{:S(2)}) collective-permute-start(s32[1,1,7,20]{3,1,2,0:T(1,128)} %param.15), channel_id=1, source_target_pairs={{0,4},{4,0},{8,12},{12,8},{16,20},{20,16},{24,28},{28,24},{1,5},{5... | collective-permute-start | bytes 1688 | tf_op jit(solution)/shard_map/ppermute | solution.py:10
  12.9 32.0 %collective-permute-start.3 = (bf16[1,1,7,20,4096]{4,2,3,1,0:T(8,128)(2,1)}, bf16[1,1,7,20,4096]{4,2,3,1,0:T(8,128)(2,1)S(1)}, u32[]{:S(2)}, u32[]{:S(2)}) collective-permute-start(bf16[1,1,7,20,4096]{4,2,3,1,0:T(8,128)(2,1)} %param.13), channel_id=1, source_target_pairs={{0,4},{4,0},{8,12},{12,8},{16,20},{20,16},{24,28},{28,24},{1,5},{5... | collective-permute-start | bytes 3440648 | tf_op jit(solution)/shard_map/ppermute | solution.py:10
  14.9 58.0 %collective-permute-start.2 = (bf16[1,1,7,20,4096]{4,2,3,1,0:T(8,128)(2,1)}, bf16[1,1,7,20,4096]{4,2,3,1,0:T(8,128)(2,1)S(1)}, u32[]{:S(2)}, u32[]{:S(2)}) collective-permute-start(bf16[1,1,7,20,4096]{4,2,3,1,0:T(8,128)(2,1)} %param.12), channel_id=1, source_target_pairs={{0,4},{4,0},{8,12},{12,8},{16,20},{20,16},{24,28},{28,24},{1,5},{5... | collective-permute-start | bytes 3440648 | tf_op jit(solution)/shard_map/ppermute | solution.py:10
  14.9 84.7 %collective-permute-start.1 = (bf16[1,1,7,20,4096]{4,2,3,1,0:T(8,128)(2,1)}, bf16[1,1,7,20,4096]{4,2,3,1,0:T(8,128)(2,1)}, u32[]{:S(2)}, u32[]{:S(2)}) collective-permute-start(bf16[1,1,7,20,4096]{4,2,3,1,0:T(8,128)(2,1)} %param.11), channel_id=1, source_target_pairs={{0,4},{4,0},{8,12},{12,8},{16,20},{20,16},{24,28},{28,24},{1,5},{5... | collective-permute-start | bytes 3440648 | tf_op jit(solution)/shard_map/ppermute | solution.py:10
  18.9 228.2 %all-reduce.3.cloned.1.call-start = ((), (), s32[]{:S(2)}) async-start(), calls=%async_computation | async-start | bytes 4194304 | tf_op jit(solution)/shard_map/psum | solution.py:89
  132.1 12.5 %slice-start = ((s8[4587520]{0:T(1024)(128)(4,1)}), s8[393216]{0:T(1024)(128)(4,1)S(1)}, s32[]{:S(2)}) async-start(s8[4587520]{0:T(1024)(128)(4,1)} %bitcast.70), calls=%async_computation.6 | async-start | bytes 786432
  136.8 7.8 %slice-start.1 = ((s8[4587520]{0:T(1024)(128)(4,1)}), s8[4194304]{0:T(1024)(128)(4,1)S(1)}, s32[]{:S(2)}) async-start(s8[4587520]{0:T(1024)(128)(4,1)} %bitcast.70), calls=%async_computation.7 | async-start | bytes 8388608
  150.8 4.7 %copy-start.1 = (bf16[7,20,64,64]{3,2,0,1:T(8,128)(2,1)S(1)}, bf16[7,20,64,64]{3,2,0,1:T(8,128)(2,1)}, u32[]{:S(2)}) copy-start(bf16[7,20,64,64]{3,2,0,1:T(8,128)(2,1)} %concatenate.51) | copy-start | bytes 3440644
  150.8 4.7 %copy-start.3 = (bf16[7,20,64,64]{3,2,0,1:T(8,128)(2,1)S(1)}, bf16[7,20,64,64]{3,2,0,1:T(8,128)(2,1)}, u32[]{:S(2)}) copy-start(bf16[7,20,64,64]{3,2,0,1:T(8,128)(2,1)} %concatenate.50) | copy-start | bytes 3440644
  150.8 6.8 %slice-start.2 = ((s8[4587520]{0:T(1024)(128)(4,1)}), s8[4194304]{0:T(1024)(128)(4,1)S(1)}, s32[]{:S(2)}) async-start(s8[4587520]{0:T(1024)(128)(4,1)} %bitcast.72), calls=%async_computation.8 | async-start | bytes 8388608
  155.6 2.0 slice-start.3
  192.6 54.5 %copy-start = (bf16[1,1,4096,128]{3,2,1,0:T(8,128)(2,1)S(1)}, bf16[1,1,4096,128]{3,2,1,0:T(8,128)(2,1)}, u32[]{:S(2)}) copy-start(bf16[1,1,4096,128]{3,2,1,0:T(8,128)(2,1)} %all-gather.9.cloned.1.call-done) | copy-start | bytes 3145732
  194.1 71.3 %all-gather.13.cloned.1.call-start = ((), (), s32[]{:S(2)}) async-start(), calls=%async_computation.4 | async-start | bytes 1310720 | tf_op jit(solution)/shard_map/all_gather | solution.py:84
  194.7 189.9 %all-reduce.5.cloned.1.call-start = ((), (), s32[]{:S(2)}) async-start(), calls=%async_computation.1 | async-start | bytes 4194304 | tf_op jit(solution)/shard_map/psum | solution.py:89
  248.9 7.4 %copy-start.5 = (bf16[4096,128]{1,0:T(8,128)(2,1)}, bf16[4096,128]{1,0:T(8,128)(2,1)S(1)}, u32[]{:S(2)}) copy-start(bf16[4096,128]{1,0:T(8,128)(2,1)S(1)} %fusion.12) | copy-start | bytes 3145732
  248.9 26.7 %collective-permute-start.5 = (bf16[4096,128]{1,0:T(8,128)(2,1)S(1)}, bf16[4096,128]{1,0:T(8,128)(2,1)S(1)}, u32[]{:S(2)}, u32[]{:S(2)}) collective-permute-start(bf16[4096,128]{1,0:T(8,128)(2,1)S(1)} %fusion.12), channel_id=1, source_target_pairs={{8,0},{12,4},{16,8},{20,12},{24,16},{28,20},{9,1},{13,5},{17,9},{2... | collective-permute-start | bytes 3145736 | tf_op jit(solution)/shard_map/ppermute | solution.py:16
  277.0 18.3 %copy-start.6 = (f32[14,128,128]{2,1,0:T(8,128)S(1)}, f32[14,128,128]{2,1,0:T(8,128)}, u32[]{:S(2)}) copy-start(f32[14,128,128]{2,1,0:T(8,128)} %fusion.16) | copy-start | bytes 2752516
  290.5 4.8 %copy-start.2 = (bf16[7,20,64,64]{3,2,0,1:T(8,128)(2,1)S(1)}, bf16[7,20,64,64]{3,2,0,1:T(8,128)(2,1)}, u32[]{:S(2)}) copy-start(bf16[7,20,64,64]{3,2,0,1:T(8,128)(2,1)} %concatenate.51) | copy-start | bytes 3440644
  290.5 4.8 %copy-start.4 = (bf16[7,20,64,64]{3,2,0,1:T(8,128)(2,1)S(1)}, bf16[7,20,64,64]{3,2,0,1:T(8,128)(2,1)}, u32[]{:S(2)}) copy-start(bf16[7,20,64,64]{3,2,0,1:T(8,128)(2,1)} %concatenate.50) | copy-start | bytes 3440644
  290.5 6.8 %slice-start.4 = ((s8[4587520]{0:T(1024)(128)(4,1)}), s8[4194304]{0:T(1024)(128)(4,1)S(1)}, s32[]{:S(2)}) async-start(s8[4587520]{0:T(1024)(128)(4,1)} %bitcast.74), calls=%async_computation.10 | async-start | bytes 8388608
  295.3 2.0 slice-start.5
Sparse Core Ops, SparseCore 0:
  8.9 19.4 all-gather.14
  29.9 16.7 all-gather.10
  48.3 16.7 all-gather.8
  194.2 52.8 all-reduce.2
  248.6 16.7 all-gather.12
  333.9 50.6 all-reduce.4
where the time goes:
time: 396 us; the launch traced here: 393 us
  waiting for transfers between devices  190 us (48%)
  other arithmetic  96.5 us (24%)
  local copies, waits for them, and re-layouts  63.1 us (16%)
  matrix products  21.5 us (5%)
  between operations  13.9 us (4%)
  starting transfers between devices  8.48 us (2%)
    psum x2, waiting for transfers between devices, per_device(): summed = lax.psum(branch, 'tensor')  102 us
    ppermute x5, waiting for transfers between devices, partner_2(): lax.ppermute(x, axis, [(i, i ^ 1 << distance) for i in range(lax.axis_siz...  67.1 us
    scatter-add x2, other arithmetic, layer_branch(): jax.ops.segment_sum(per_slot.reshape(columns * slot_depth, BLK, tokens_no...  59.4 us
    gather x4, local copies, waits for them, and re-layouts, gather_tiles(): picked = jnp.take(source, jnp.maximum(row_ids, 0).reshape(-1), axis=0)  27.5 us
    concatenate x7, local copies, waits for them, and re-layouts, per_device(): jnp.concatenate([first_half[0, 0], second_half[0, 0]], axis=0)  26.3 us
    select_n x3, other arithmetic, gather_tiles(): picked = jnp.where(filled[:, None, None], picked, jnp.zeros_like(picked))  17.3 us
    ppermute x1, waiting for transfers between devices, from_behind(): return lax.ppermute(block, axis, route)  10.2 us
    dot_general x2, matrix products, layer_branch(): jnp.einsum('crkj,cjt->crkt', paired_grid, d_both, preferred_element_type=...  9.89 us
  transfers between devices with their start and end apart: 12, of which 7 were waited for; matrix products, arithmetic and copies ran while one was open for 18% of the time, Pallas kernels for 0%

commit v1 on v0

v1 whole, which is shorter than its diff:
```python
import functools

import jax
import jax.numpy as jnp
from jax import lax
from jax.experimental import pallas as pl
from jax.experimental.pallas import tpu as pltpu
from jax.sharding import PartitionSpec as P

BLK = 64
BF16 = jnp.bfloat16
F32 = jnp.float32
MESH = pl.DeviceIdType.MESH


def kernel(
    n_pipe, n_tensor,
    gate_inv, down_inv, x_ref, seed_ref, pair_ref, down_ref, out_ref,
    xs, cs, w_nat, w_tr, w_down, gu, dh, dboth, sib_out, sib_in, red_out, red_in, own, arrived,
    ag_send, ag_recv, fw_send, fw_recv, sib_send_sem, sib_recv_sem, red_send_sem, red_recv_sem, z_send, z_recv,
):
    steps, rows, tok = x_ref.shape
    cols = w_nat.shape[1] // (2 * BLK)
    slots = pair_ref.shape[0] // cols
    half = n_tensor // 2
    chips = 2 * half
    p = lax.axis_index("pipe")
    t = lax.axis_index("tensor")
    ph, core, tc = p % 2, t % 2, t // 2
    base = p - ph
    has_next = p + 2 < n_pipe
    has_prev = p >= 2

    def at(dph, dtc, other=0):
        return (ph + dph) % 2, (tc + dtc) % half, (core + other) % 2

    def dev(dph, dtc):
        q, c, k = at(dph, dtc)
        return (base + q, c * 2 + k)

    sibling = (p, tc * 2 + (core + 1) % 2)
    peers = [(a, b) for b in range(half) for a in range(2) if a or b]
    order = [(a, b) for b in range(half) for a in range(2)]

    barrier = pltpu.get_barrier_semaphore()
    for a, b in peers:
        pl.semaphore_signal(barrier, inc=1, device_id=dev(a, b), device_id_type=MESH)
    pl.semaphore_signal(barrier, inc=1, device_id=sibling, device_id_type=MESH)

    @pl.when(has_next)
    def _():
        pl.semaphore_signal(barrier, inc=1, device_id=(p + 2, t), device_id_type=MESH)

    @pl.when(has_prev)
    def _():
        pl.semaphore_signal(barrier, inc=1, device_id=(p - 2, t), device_id_type=MESH)

    neighbours = chips + jnp.where(has_next, 1, 0) + jnp.where(has_prev, 1, 0)
    pl.semaphore_wait(barrier, neighbours)

    pending = []

    def slot(buf, q, c, k):
        return buf.at[
            pl.ds(pl.multiple_of((c * 2 + k) * rows, rows), rows),
            pl.ds(pl.multiple_of(q * tok, tok), tok),
        ]

    def remote(src, dst, s_sem, r_sem, device):
        return pltpu.make_async_remote_copy(
            src_ref=src, dst_ref=dst, send_sem=s_sem, recv_sem=r_sem, device_id=device, device_id_type=MESH
        )

    def gather_start(n, buf, src):
        mine = slot(buf, ph, tc, core)
        for a, b in peers:
            cp = remote(src, mine, ag_send.at[n, a * half + b], ag_recv.at[n, a * half + b], dev(a, b))
            cp.start()
            pending.append(cp)
        cp = remote(src, mine, fw_send.at[n, 0], fw_recv.at[n, 0], sibling)
        cp.start()
        pending.append(cp)
        buf[
            pl.ds(pl.multiple_of(t * rows, rows), rows), pl.ds(pl.multiple_of(ph * tok, tok), tok)
        ] = src[...]

    def gather_forward(n, buf):
        for a, b in peers:
            i = a * half + b
            got = slot(buf, *at(-a, -b))
            remote(got, got, ag_send.at[n, i], ag_recv.at[n, i], dev(a, b)).wait_recv()
            cp = remote(got, got, fw_send.at[n, i], fw_recv.at[n, i], sibling)
            cp.start()
            pending.append(cp)

    def gather_wait(n, buf):
        for a, b in order:
            i = a * half + b
            got = slot(buf, *at(-a, -b, 1))
            remote(got, got, fw_send.at[n, i], fw_recv.at[n, i], sibling).wait_recv()

    gather_start(0, xs.at[0], x_ref.at[0])
    gather_start(1, cs.at[0], seed_ref.at[0])

    lane_low = lax.broadcasted_iota(jnp.int32, (BLK, 2 * BLK), 1) < BLK
    zero = jnp.zeros((BLK, 2 * BLK), BF16)

    def build(lo, hi):
        def body(j, carry):
            at_row = pl.multiple_of(j * 2 * BLK, 2 * BLK)
            for c in range(cols):
                parts = []
                for e in range(2):
                    i = gate_inv[c, j * 2 + e]
                    tile = pair_ref[c * slots + jnp.maximum(i, 0)]
                    parts.append(jnp.where(i >= 0, tile, zero))
                block = jnp.concatenate(parts, axis=0)
                w_nat[pl.ds(at_row, 2 * BLK), c * 2 * BLK : (c + 1) * 2 * BLK] = block
                w_tr[c * 2 * BLK : (c + 1) * 2 * BLK, pl.ds(at_row, 2 * BLK)] = block.T
                i0 = down_inv[c, j * 2]
                i1 = down_inv[c, j * 2 + 1]
                t0 = jnp.where(i0 >= 0, down_ref[c * slots + jnp.maximum(i0, 0)], zero)
                t1 = jnp.where(i1 >= 0, down_ref[c * slots + jnp.maximum(i1, 0)], zero)
                w_down[c * BLK : (c + 1) * BLK, pl.ds(at_row, 2 * BLK)] = jnp.where(lane_low, t0, t1)
            return carry

        lax.fori_loop(lo, hi, body, 0)

    total = w_nat.shape[0] // (2 * BLK)
    build(0, total // 2)
    gather_forward(0, xs.at[0])
    for n in range(1, steps):
        gather_start(1 + n, xs.at[n], x_ref.at[n])
    build(total // 2, total)
    gather_forward(1, cs.at[0])

    def forward(n):
        gu[n] = jnp.zeros(gu.shape[1:], F32)

        def body(j, carry):
            r = pl.ds(pl.multiple_of(j * rows, rows), rows)
            gu[n] += jnp.dot(w_tr[:, r], xs[n, r, :], preferred_element_type=F32)
            return carry

        lax.fori_loop(0, n_tensor, body, 0)

    def hidden(n):
        dh[...] = jnp.zeros(dh.shape, F32)

        def body(j, carry):
            r = pl.ds(pl.multiple_of(j * rows, rows), rows)
            dh[...] += jnp.dot(w_down[:, r], cs[n, r, :], preferred_element_type=F32)
            return carry

        lax.fori_loop(0, n_tensor, body, 0)

        def act(c, carry):
            r2 = pl.multiple_of(c * 2 * BLK, 2 * BLK)
            g = gu[n, pl.ds(r2, BLK), :]
            u = gu[n, pl.ds(r2 + BLK, BLK), :]
            d = dh[pl.ds(pl.multiple_of(c * BLK, BLK), BLK), :]
            s = jax.nn.sigmoid(g)
            dboth[pl.ds(r2, BLK), :] = (d * u * s * (1.0 + g * (1.0 - s))).astype(BF16)
            dboth[pl.ds(r2 + BLK, BLK), :] = (d * g * s).astype(BF16)
            return carry

        lax.fori_loop(0, cols, act, 0)

    def branch(c, k):
        r = pl.ds(pl.multiple_of((c * 2 + k) * rows, rows), rows)
        return jnp.dot(w_nat[r, :], dboth[...], preferred_element_type=F32)

    def reduce_start(n):
        for b in list(range(1, half)) + [0]:
            _, c, k = at(0, b, 1)
            sib_out[n, b] = branch(c, k).astype(BF16)
            cp = remote(sib_out.at[n, b], sib_in.at[n, b], sib_send_sem.at[n, b], sib_recv_sem.at[n, b], sibling)
            cp.start()
            pending.append(cp)
        for b in list(range(1, half)) + [0]:
            _, c, k = at(0, b)
            part = branch(c, k)
            remote(
                sib_out.at[n, b], sib_in.at[n, b], sib_send_sem.at[n, b], sib_recv_sem.at[n, b], sibling
            ).wait_recv()
            part = part + sib_in[n, b].astype(F32)
            red_out[n, b] = part.astype(BF16)
            if b == 0:
                own[...] = part
            for a in range(2):
                if a or b:
                    q = (ph + a) % 2
                    cp = remote(
                        red_out.at[n, b, :, pl.ds(pl.multiple_of(q * tok, tok), tok)],
                        red_in.at[n, a * half + b],
                        red_send_sem.at[n, a * half + b],
                        red_recv_sem.at[n, a * half + b],
                        dev(a, b),
                    )
                    cp.start()
                    pending.append(cp)

    def reduce_finish(n, cot):
        acc = own[:, pl.ds(pl.multiple_of(ph * tok, tok), tok)]
        for a, b in peers:
            i = a * half + b
            remote(
                red_in.at[n, i], red_in.at[n, i], red_send_sem.at[n, i], red_recv_sem.at[n, i], dev(a, b)
            ).wait_recv()
            acc = acc + red_in[n, i].astype(F32)
        out_ref[n] = (cot.astype(F32) + acc).astype(BF16)

    gather_wait(0, xs.at[0])
    forward(0)
    gather_wait(1, cs.at[0])
    for n in range(steps):
        hidden(n)
        reduce_start(n)
        if n + 1 < steps:
            gather_forward(2 + n, xs.at[n + 1])
            gather_wait(2 + n, xs.at[n + 1])
            forward(n + 1)
        reduce_finish(n, seed_ref[0] if n == 0 else arrived[n - 1])
        if n + 1 < steps:
            hop = remote(out_ref.at[n], arrived.at[n], z_send.at[n], z_recv.at[n], (p - 2, t))

            @pl.when(has_prev)
            def _():
                hop.start()

            @pl.when(has_next)
            def _():
                hop.wait_recv()

            @pl.when(jnp.logical_not(has_next))
            def _():
                arrived[n] = seed_ref[n + 1]

            gather_start(steps + 1 + n, cs.at[n + 1], arrived.at[n])
            gather_forward(steps + 1 + n, cs.at[n + 1])
            gather_wait(steps + 1 + n, cs.at[n + 1])

            @pl.when(has_prev)
            def _():
                hop.wait_send()

    for cp in pending:
        cp.wait_send()


def per_device(n_pipe, n_tensor, x_saved, seed_grad, gate_blocks, up_blocks, down_blocks, gate_rows, down_rows):
    _, steps, rows, tok = x_saved.shape
    cols, slots = gate_rows.shape[2:]
    width = rows * n_tensor
    half = n_tensor // 2

    def inverse(ids):
        hit = ids[0, 0][:, :, None] == jnp.arange(width // BLK, dtype=jnp.int32)
        return jnp.max(jnp.where(hit, jnp.arange(slots, dtype=jnp.int32)[None, :, None], -1), axis=1)

    shape = (cols * slots, BLK, BLK)
    pair = jnp.concatenate([gate_blocks.reshape(shape), up_blocks.reshape(shape)], axis=2)
    down = down_blocks.reshape(shape)
    down = jnp.concatenate([down, down], axis=2)
    hid = cols * BLK
    gathers = 2 * steps
    dma = pltpu.SemaphoreType.DMA
    out = pl.pallas_call(
        functools.partial(kernel, n_pipe, n_tensor),
        out_shape=jax.ShapeDtypeStruct((steps, rows, tok), BF16),
        in_specs=[pl.BlockSpec(memory_space=pltpu.SMEM)] * 2 + [pl.BlockSpec(memory_space=pltpu.VMEM)] * 4,
        out_specs=pl.BlockSpec(memory_space=pltpu.VMEM),
        scratch_shapes=[
            pltpu.VMEM((steps, width, 2 * tok), BF16),
            pltpu.VMEM((steps, width, 2 * tok), BF16),
            pltpu.VMEM((width, 2 * hid), BF16),
            pltpu.VMEM((2 * hid, width), BF16),
            pltpu.VMEM((hid, width), BF16),
            pltpu.VMEM((steps, 2 * hid, 2 * tok), F32),
            pltpu.VMEM((hid, 2 * tok), F32),
            pltpu.VMEM((2 * hid, 2 * tok), BF16),
            pltpu.VMEM((steps, half, rows, 2 * tok), BF16),
            pltpu.VMEM((steps, half, rows, 2 * tok), BF16),
            pltpu.VMEM((steps, half, rows, 2 * tok), BF16),
            pltpu.VMEM((steps, n_tensor, rows, tok), BF16),
            pltpu.VMEM((rows, 2 * tok), F32),
            pltpu.VMEM((steps - 1, rows, tok), BF16),
            dma((gathers, n_tensor)),
            dma((gathers, n_tensor)),
            dma((gathers, n_tensor)),
            dma((gathers, n_tensor)),
            dma((steps, half)),
            dma((steps, half)),
            dma((steps, n_tensor)),
            dma((steps, n_tensor)),
            dma((steps,)),
            dma((steps,)),
        ],
        compiler_params=pltpu.CompilerParams(
            collective_id=0, has_side_effects=True, vmem_limit_bytes=58 * 1024 * 1024
        ),
    )(inverse(gate_rows), inverse(down_rows), x_saved[0], seed_grad[0], pair, down)
    return out[None]


def solution(mesh):
    return jax.shard_map(
        functools.partial(per_device, mesh.shape["pipe"], mesh.shape["tensor"]),
        mesh=mesh,
        in_specs=(
            P("pipe", None, "tensor", None),
            P("pipe", None, "tensor", None),
            P("pipe", "tensor", None, None, None),
            P("pipe", "tensor", None, None, None),
            P("pipe", "tensor", None, None, None),
            P("pipe", "tensor", None, None),
            P("pipe", "tensor", None, None),
        ),
        out_specs=P("pipe", None, "tensor", None),
        check_vma=False,
    )
```

time: 396 us -> 130 us (0.33)
  waiting for transfers between devices: 190 us -> 0 us
  Pallas kernels: 0 us -> 98.1 us
  other arithmetic: 96.5 us -> 7.43 us
  local copies, waits for them, and re-layouts: 63.1 us -> 24.4 us
  matrix products: 21.5 us -> 0 us
  between operations: 13.9 us -> 0.02 us
  starting transfers between devices: 8.48 us -> 0 us
    psum x2 -> x0, waiting for transfers between devices: 102 us -> none  [per_device(): summed = lax.psum(branch, 'tensor')]
    pallas_call x0 -> x1, Pallas kernels: none -> 98.1 us  [per_device(): pl.pallas_call(functools.partial(kernel, n_pipe, n_tensor), out_shape=jax...]
    ppermute x6 -> x0, waiting for transfers between devices: 77.3 us -> none  [the longest x5 67.1 us: partner_2(): lax.ppermute(x, axis, [(i, i ^ 1 << distance) for i in range(lax.axis_siz...]
    scatter-add x2 -> x0, other arithmetic: 59.4 us -> none  [layer_branch(): jax.ops.segment_sum(per_slot.reshape(columns * slot_depth, BLK, tokens_no...]
    gather x4 -> x0, local copies, waits for them, and re-layouts: 27.5 us -> none  [gather_tiles(): picked = jnp.take(source, jnp.maximum(row_ids, 0).reshape(-1), axis=0)]
    concatenate x7 -> x0, local copies, waits for them, and re-layouts: 26.3 us -> none  [per_device(): jnp.concatenate([first_half[0, 0], second_half[0, 0]], axis=0)]
    select_n x10 -> x0, other arithmetic: 26.2 us -> none  [the longest x3 17.3 us: gather_tiles(): picked = jnp.where(filled[:, None, None], picked, jnp.zeros_like(picked))]
    dot_general x6 -> x0, matrix products: 21.5 us -> none  [the longest x2 9.89 us: layer_branch(): jnp.einsum('crkj,cjt->crkt', paired_grid, d_both, preferred_element_type=...]
  transfers between devices with their start and end apart: 12 -> 0, of which waited for: 7 -> 0; matrix products, arithmetic and copies ran while one was open for 18% -> 0% of each run, Pallas kernels for 0% -> 0%
where the time goes in v1:
time: 130 us
  Pallas kernels  98.1 us (75%)
  local copies, waits for them, and re-layouts  24.4 us (19%)
  other arithmetic  7.43 us (6%)
    pallas_call x1, Pallas kernels, per_device(): pl.pallas_call(functools.partial(kernel, n_pipe, n_tensor), out_shape=jax...  98.1 us
    unnamed x8, local copies, waits for them, and re-layouts  11.3 us
    concatenate x1, other arithmetic, per_device(): jnp.concatenate([gate_blocks.reshape(shape), up_blocks.reshape(shape)], a...  6.72 us
    reshape x1, local copies, waits for them, and re-layouts, per_device(): down = down_blocks.reshape(shape)  4.65 us
    reshape x1, local copies, waits for them, and re-layouts, per_device(): up_blocks.reshape(shape)  4.63 us
    reshape x1, local copies, waits for them, and re-layouts, per_device(): gate_blocks.reshape(shape)  3.65 us

profile of v1, /device:TPU:0, one launch (start us, length us, event | category | flops | bytes accessed | tf_op | source)
XLA Modules:
  0.0 130.0 jit_solution(1924704557016923827)
XLA Ops:
  0.0 3.1 %copy.16 = bf16[1,1,7,20,4096]{4,3,2,1,0:T(8,128)(2,1)} copy(bf16[1,1,7,20,4096]{4,2,3,1,0:T(8,128)(2,1)} %param.9) | data formatting | bytes 2293760 | tf_op args[2]
  3.1 3.7 %reshape.11 = bf16[140,64,64]{2,1,0:T(8,128)(2,1)S(1)} reshape(bf16[1,1,7,20,4096]{4,3,2,1,0:T(8,128)(2,1)} %copy.16) | data formatting | bytes 2293760 | tf_op jit(solution)/shard_map/reshape | solution.py:262
  6.8 3.1 %copy.17 = bf16[1,1,7,20,4096]{4,3,2,1,0:T(8,128)(2,1)} copy(bf16[1,1,7,20,4096]{4,2,3,1,0:T(8,128)(2,1)} %param.10) | data formatting | bytes 2293760 | tf_op args[3]
  9.9 4.6 %reshape.12 = bf16[140,64,64]{2,1,0:T(8,128)(2,1)} reshape(bf16[1,1,7,20,4096]{4,3,2,1,0:T(8,128)(2,1)} %copy.17) | data formatting | bytes 2293760 | tf_op jit(solution)/shard_map/reshape | solution.py:262
  14.6 3.1 %copy.18 = bf16[1,1,7,20,4096]{4,3,2,1,0:T(8,128)(2,1)} copy(bf16[1,1,7,20,4096]{4,2,3,1,0:T(8,128)(2,1)} %param.11) | data formatting | bytes 2293760 | tf_op args[4]
  17.7 4.7 %reshape.13 = bf16[140,64,64]{2,1,0:T(8,128)(2,1)} reshape(bf16[1,1,7,20,4096]{4,3,2,1,0:T(8,128)(2,1)} %copy.18) | data formatting | bytes 2293760 | tf_op jit(solution)/shard_map/reshape | solution.py:263
  22.4 0.0 copy-start
  22.4 0.0 copy-start.1
  22.4 6.7 %pad_maximum_fusion = (bf16[140,64,128]{2,1,0:T(8,128)(2,1)}, bf16[140,64,128]{2,1,0:T(8,128)(2,1)}) fusion(bf16[140,64,64]{2,1,0:T(8,128)(2,1)} %reshape.12, bf16[140,64,64]{2,1,0:T(8,128)(2,1)S(1)} %reshape.11, bf16[140,64,64]{2,1,0:T(8,128)(2,1)} %reshape.13), kind=kLoop, calls=%fused_computation | loop fusion | flops 9175040 | bytes 8028160 | tf_op jit(solution)/shard_map/concatenate | solution.py:262
  29.1 0.0 copy-done
  29.1 0.1 copy.19
  29.2 0.0 copy-done.1
  29.2 0.1 copy.20
  29.3 0.7 select_reduce_fusion
  30.0 98.1 %shard_map.73 = bf16[2,1024,128]{2,1,0:T(8,128)(2,1)} custom-call(s32[7,64]{1,0:T(8,128)} %get-tuple-element.8.gate_inv, s32[7,64]{1,0:T(8,128)} %get-tuple-element.7.down_inv, bf16[2,1024,128]{2,1,0:T(8,128)(2,1)} %bitcast.6, bf16[2,1024,128]{2,1,0:T(8,128)(2,1)} %bitcast.7, bf16[140,64,128]{2,1,0:T(8,128)(2,1)} %get-tuple-element.5.pair_ref, ...), custom_call_target="tpu_custom_call" | custom-call | tf_op jit(solution)/shard_map/pallas_call | solution.py:268
  128.1 1.9 %copy.22 = bf16[1,2,1024,128]{3,2,1,0:T(8,128)(2,1)} copy(bf16[1,2,1024,128]{3,2,1,0:T(8,128)(2,1)} %bitcast.5) | data formatting | bytes 1048576
Async XLA Ops:
  22.4 6.7 %copy-start = (s32[1,1,7,20]{3,1,2,0:T(1,128)S(1)}, s32[1,1,7,20]{3,1,2,0:T(1,128)}, u32[]{:S(2)}) copy-start(s32[1,1,7,20]{3,1,2,0:T(1,128)} %param.12) | copy-start | bytes 1684
  22.4 6.8 %copy-start.1 = (s32[1,1,7,20]{3,1,2,0:T(1,128)S(1)}, s32[1,1,7,20]{3,1,2,0:T(1,128)}, u32[]{:S(2)}) copy-start(s32[1,1,7,20]{3,1,2,0:T(1,128)} %param.13) | copy-start | bytes 1684

commit v2 on v1

--- a/solution.py
+++ b/solution.py
@@ -129,10 +129,10 @@
     total = w_nat.shape[0] // (2 * BLK)
     build(0, total // 2)
     gather_forward(0, xs.at[0])
+    build(total // 2, total)
+    gather_forward(1, cs.at[0])
     for n in range(1, steps):
         gather_start(1 + n, xs.at[n], x_ref.at[n])
-    build(total // 2, total)
-    gather_forward(1, cs.at[0])
 
     def forward(n):
         gu[n] = jnp.zeros(gu.shape[1:], F32)
@@ -248,6 +248,54 @@
         cp.wait_send()
 
 
+def untangle(gate_ref, up_ref, down_ref, pair_ref, twin_ref, a_ref, b_ref):
+    slots = gate_ref.shape[1]
+    deep = BLK // 2
+    low = lax.broadcasted_iota(jnp.int32, (deep, 2 * BLK), 1) < BLK
+
+    def spread(src, dst):
+        for k in range(deep):
+            piece = src[0, :, k * 2 * BLK : (k + 1) * 2 * BLK].astype(F32)
+            dst[pl.ds(k, slots, stride=deep), :] = piece
+
+    def weave(left, right, out, tmp):
+        def body(r, carry):
+            rows = pl.ds(pl.multiple_of(r * deep, deep), deep)
+            a = left[rows, :]
+            b = right[rows, :]
+            even = jnp.where(low, a, pltpu.roll(b, BLK, 1))
+            odd = jnp.where(low, pltpu.roll(a, BLK, 1), b)
+            tmp[pl.ds(0, deep, stride=2), :] = even
+            tmp[pl.ds(1, deep, stride=2), :] = odd
+            out[r] = tmp[...].astype(BF16)
+            return carry
+
+        lax.fori_loop(0, slots, body, 0, unroll=4)
+
+    def run(tmp):
+        spread(gate_ref, a_ref)
+        spread(up_ref, b_ref)
+        weave(a_ref, b_ref, pair_ref, tmp)
+        spread(down_ref, a_ref)
+        weave(a_ref, a_ref, twin_ref, tmp)
+
+    pl.run_scoped(run, pltpu.VMEM((BLK, 2 * BLK), F32))
+
+
+def tiles_of(gate_blocks, up_blocks, down_blocks):
+    cols, slots, flat = gate_blocks.shape
+    tile = jax.ShapeDtypeStruct((cols * slots, BLK, 2 * BLK), BF16)
+    room = pltpu.VMEM(((slots + 7) // 8 * 8 * (BLK // 2) + BLK, 2 * BLK), F32)
+    return pl.pallas_call(
+        untangle,
+        grid=(cols,),
+        in_specs=[pl.BlockSpec((1, slots, flat), lambda c: (c, 0, 0))] * 3,
+        out_specs=[pl.BlockSpec((slots, BLK, 2 * BLK), lambda c: (c, 0, 0))] * 2,
+        out_shape=[tile, tile],
+        scratch_shapes=[room, room],
+    )(gate_blocks, up_blocks, down_blocks)
+
+
 def per_device(n_pipe, n_tensor, x_saved, seed_grad, gate_blocks, up_blocks, down_blocks, gate_rows, down_rows):
     _, steps, rows, tok = x_saved.shape
     cols, slots = gate_rows.shape[2:]
@@ -258,10 +306,7 @@
         hit = ids[0, 0][:, :, None] == jnp.arange(width // BLK, dtype=jnp.int32)
         return jnp.max(jnp.where(hit, jnp.arange(slots, dtype=jnp.int32)[None, :, None], -1), axis=1)
 
-    shape = (cols * slots, BLK, BLK)
-    pair = jnp.concatenate([gate_blocks.reshape(shape), up_blocks.reshape(shape)], axis=2)
-    down = down_blocks.reshape(shape)
-    down = jnp.concatenate([down, down], axis=2)
+    pair, down = tiles_of(gate_blocks[0, 0], up_blocks[0, 0], down_blocks[0, 0])
     hid = cols * BLK
     gathers = 2 * steps
     dma = pltpu.SemaphoreType.DMA

time: 130 us -> 124 us (0.954)
  Pallas kernels: 98.1 us -> 114 us
  local copies, waits for them, and re-layouts: 24.4 us -> 8.74 us
  other arithmetic: 7.43 us -> 0.71 us
    pallas_call x0 -> x1, Pallas kernels: none -> 15.5 us  [tiles_of(): pl.pallas_call(untangle, grid=(cols,), in_specs=[pl.BlockSpec((1, slots,...]
    reshape x3 -> x0, local copies, waits for them, and re-layouts: 12.9 us -> none  [the longest x1 4.65 us: per_device(): down = down_blocks.reshape(shape)]
    unnamed x8, local copies, waits for them, and re-layouts: 11.3 us -> 3.72 us
    concatenate x1 -> x0, other arithmetic: 6.72 us -> none  [per_device(): jnp.concatenate([gate_blocks.reshape(shape), up_blocks.reshape(shape)], a...]
    squeeze x0 -> x1, local copies, waits for them, and re-layouts: none -> 4.83 us  [per_device(): pair, down = tiles_of(gate_blocks[0, 0], up_blocks[0, 0], down_blocks[0, 0])]
where the time goes in v2:
time: 124 us; the launch traced here: 123 us
  Pallas kernels  114 us (92%)
  local copies, waits for them, and re-layouts  8.74 us (7%)
    pallas_call x1, Pallas kernels, per_device(): pl.pallas_call(functools.partial(kernel, n_pipe, n_tensor), out_shape=jax...  98.4 us
    pallas_call x1, Pallas kernels, tiles_of(): pl.pallas_call(untangle, grid=(cols,), in_specs=[pl.BlockSpec((1, slots,...  15.5 us
    squeeze x1, local copies, waits for them, and re-layouts, per_device(): pair, down = tiles_of(gate_blocks[0, 0], up_blocks[0, 0], down_blocks[0, 0])  4.83 us
    unnamed x8, local copies, waits for them, and re-layouts  3.72 us

profile of v2, /device:TPU:0, one launch (start us, length us, event | category | flops | bytes accessed | tf_op | source)
XLA Modules:
  0.0 123.3 jit_solution(4265656335676611767)
XLA Ops:
  0.0 0.0 copy-start
  0.0 4.8 %copy_bitcast_fusion = (bf16[7,20,4096]{2,1,0:T(8,128)(2,1)}, bf16[7,20,4096]{2,1,0:T(8,128)(2,1)}) fusion(bf16[1,1,7,20,4096]{4,2,3,1,0:T(8,128)(2,1)} %param.11, bf16[1,1,7,20,4096]{4,2,3,1,0:T(8,128)(2,1)} %param.10), kind=kLoop, calls=%fused_computation | loop fusion | bytes 4587520 | tf_op jit(solution)/shard_map/squeeze | solution.py:309
  4.8 0.0 copy-done
  4.8 1.8 %copy.21 = bf16[1,1,7,20,4096]{4,3,2,1,0:T(8,128)(2,1)} copy(bf16[1,1,7,20,4096]{4,2,3,1,0:T(8,128)(2,1)S(1)} %copy-done) | data formatting | bytes 2293760 | tf_op args[2]
  6.7 0.0 copy-start.1
  6.7 0.0 copy-start.2
  6.7 15.5 %shard_map.73 = (bf16[140,64,128]{2,1,0:T(8,128)(2,1)}, bf16[140,64,128]{2,1,0:T(8,128)(2,1)}) custom-call(bf16[7,20,4096]{2,1,0:T(8,128)(2,1)} %bitcast.12, bf16[7,20,4096]{2,1,0:T(8,128)(2,1)} %get-tuple-element.10.up_ref, bf16[7,20,4096]{2,1,0:T(8,128)(2,1)} %get-tuple-element.9.down_ref), custom_call_target="tpu_custom_call" | custom-call | tf_op jit(solution)/shard_map/pallas_call | solution.py:289
  22.2 0.0 copy-done.1
  22.2 0.1 copy.16
  22.3 0.0 copy-done.2
  22.3 0.1 copy.17
  22.4 0.7 select_reduce_fusion
  23.1 98.4 %shard_map.74 = bf16[2,1024,128]{2,1,0:T(8,128)(2,1)} custom-call(s32[7,64]{1,0:T(8,128)} %get-tuple-element.12.gate_inv, s32[7,64]{1,0:T(8,128)} %get-tuple-element.11.down_inv, bf16[2,1024,128]{2,1,0:T(8,128)(2,1)} %bitcast.14, bf16[2,1024,128]{2,1,0:T(8,128)(2,1)} %bitcast.15, bf16[140,64,128]{2,1,0:T(8,128)(2,1)} %get-tuple-element.7.pair_ref, ...), custom_call_target="tpu_custom_call" | custom-call | tf_op jit(solution)/shard_map/pallas_call | solution.py:313
  121.5 1.9 %copy.23 = bf16[1,2,1024,128]{3,2,1,0:T(8,128)(2,1)} copy(bf16[1,2,1024,128]{3,2,1,0:T(8,128)(2,1)} %bitcast.13) | data formatting | bytes 1048576
Async XLA Ops:
  0.0 4.8 %copy-start = (bf16[1,1,7,20,4096]{4,2,3,1,0:T(8,128)(2,1)S(1)}, bf16[1,1,7,20,4096]{4,2,3,1,0:T(8,128)(2,1)}, u32[]{:S(2)}) copy-start(bf16[1,1,7,20,4096]{4,2,3,1,0:T(8,128)(2,1)} %param.9) | copy-start | bytes 3440644
  6.7 15.5 %copy-start.1 = (s32[1,1,7,20]{3,1,2,0:T(1,128)S(1)}, s32[1,1,7,20]{3,1,2,0:T(1,128)}, u32[]{:S(2)}) copy-start(s32[1,1,7,20]{3,1,2,0:T(1,128)} %param.12) | copy-start | bytes 1684
  6.7 15.6 %copy-start.2 = (s32[1,1,7,20]{3,1,2,0:T(1,128)S(1)}, s32[1,1,7,20]{3,1,2,0:T(1,128)}, u32[]{:S(2)}) copy-start(s32[1,1,7,20]{3,1,2,0:T(1,128)} %param.13) | copy-start | bytes 1684
